TPU v7x, 128 devices: a whole 4x4x4 slice. The times are simulated.
128 devices in a mesh: subj: 4 (over z_hi, core), depth: 32 (over y, z_lo, x).
Axes of the slice: x: 4, y: 4, z: 4 (z_hi: 2, z_lo: 2; z = z_hi * 2 + z_lo), core: 2. Of those that a mesh axis runs over, the one named last changes fastest.
Arguments:
- volumes: bfloat16 [4, 256, 256, 256], P('subj', 'depth'), may hold values from -6 to 6
- depth_shift: int32 [4, 32], P('subj', 'depth'), may hold values from -8 to 7
- plane_shift: int32 [4, 32, 2], P('subj', 'depth'), may hold values from -4 to 3
- fraction_steps: int32 [4, 32, 3], P('subj', 'depth'), may hold values from 0 to 3
Outputs:
- velocity: bfloat16 [4, 3, 256, 256, 256], P('subj', None, 'depth')
- template: bfloat16 [256, 256, 256], P('depth')
All inputs are finite; a program needn't handle non-finite values.
Results may differ from a plain program's by a relative error of at most 0.018.
Values may be sent and summed in bfloat16 or wider, within the bound.
A program may use at most 128 MiB of HBM per device.

v0:
```python
import math

import jax
import jax.numpy as jnp
from jax import lax
from jax.sharding import PartitionSpec as P

BRICK = 8
MAXIN = 4


eps = 1e-05


def padded_2(cells, sides, width):
    for axis, dim in sides:
        count = lax.axis_size(axis)
        ends = count - 1
        head = lax.slice_in_dim(cells, 0, width, axis=dim)
        tail = lax.slice_in_dim(cells, cells.shape[dim] - width, cells.shape[dim], axis=dim)
        cells = jnp.concatenate(
            [
                lax.ppermute(tail, axis, [(i, (i + 1) % count) for i in range(ends)]),
                cells,
                lax.ppermute(head, axis, [((i + 1) % count, i) for i in range(ends)]),
            ],
            axis=dim,
        )
    return cells


def shift_lerp(field, offset, frac, axis):
    count = field.shape[axis]
    widths = [(0, 0)] * field.ndim
    widths[axis] = (MAXIN, MAXIN)
    padded = jnp.pad(field, widths)
    part = lax.dynamic_slice_in_dim(padded, offset + MAXIN, count + 1, axis)
    lower = lax.slice_in_dim(part, 0, count, axis=axis)
    upper = lax.slice_in_dim(part, 1, count + 1, axis=axis)
    return lower * (1.0 - frac) + upper * frac


def warp_subject(padded, shifts, planes, steps):
    bricks = shifts.shape[0]
    starts = jnp.arange(bricks, dtype=jnp.int32) * BRICK + BRICK + shifts

    def one_brick(start, plane, step):
        rows = lax.dynamic_slice_in_dim(padded, start, BRICK + 1, 0).astype(jnp.float32)
        fracs = step.astype(jnp.float32) / 4.0
        inner = rows[:-1] * (1.0 - fracs[0]) + rows[1:] * fracs[0]
        inner = shift_lerp(inner, plane[0], fracs[1], 1)
        inner = shift_lerp(inner, plane[1], fracs[2], 2)
        return inner

    blocks = jax.vmap(one_brick)(starts, planes, steps)
    return blocks.reshape((bricks * BRICK,) + blocks.shape[2:]).astype(jnp.bfloat16)


def box_sum(field):
    count = field.shape[0] - 4
    height, width = (field.shape[1], field.shape[2])
    total = field[0:count]
    for k in range(1, 5):
        total = total + field[k : k + count]
    padded = jnp.pad(total, ((0, 0), (2, 2), (0, 0)))
    total = padded[:, 0:height]
    for k in range(1, 5):
        total = total + padded[:, k : k + height]
    padded = jnp.pad(total, ((0, 0), (0, 0), (2, 2)))
    total = padded[:, :, 0:width]
    for k in range(1, 5):
        total = total + padded[:, :, k : k + width]
    return total


def force_of(image, templ):
    count = image.shape[0] - 4
    mean_i = box_sum(image) / 125.0
    mean_j = box_sum(templ) / 125.0
    cross = box_sum(image * templ) / 125.0 - mean_i * mean_j
    var_i = box_sum(image * image) / 125.0 - mean_i * mean_i + eps
    var_j = box_sum(templ * templ) / 125.0 - mean_j * mean_j + eps
    inner_i = image[2 : 2 + count]
    inner_j = templ[2 : 2 + count]
    factor = 2.0 * cross / (var_i * var_j)
    differ = inner_j - mean_j - cross / var_i * (inner_i - mean_i)
    grad_z = (image[3 : 3 + count] - image[1 : 1 + count]) * 0.5
    padded = jnp.pad(inner_i, ((0, 0), (1, 1), (0, 0)))
    grad_y = (padded[:, 2:] - padded[:, :-2]) * 0.5
    padded = jnp.pad(inner_i, ((0, 0), (0, 0), (1, 1)))
    grad_x = (padded[:, :, 2:] - padded[:, :, :-2]) * 0.5
    common = factor * differ
    return jnp.stack([common * grad_z, common * grad_y, common * grad_x])


def gauss_taps():
    raw = [math.exp(-(t * t) / 4.5) for t in range(-4, 5)]
    total = sum(raw)
    return [r / total for r in raw]


def smooth(field):
    taps = gauss_taps()
    count = field.shape[1] - 8
    height, width = (field.shape[2], field.shape[3])
    total = taps[0] * field[:, 0:count]
    for k in range(1, 9):
        total = total + taps[k] * field[:, k : k + count]
    padded = jnp.pad(total, ((0, 0), (0, 0), (4, 4), (0, 0)))
    total = taps[0] * padded[:, :, 0:height]
    for k in range(1, 9):
        total = total + taps[k] * padded[:, :, k : k + height]
    padded = jnp.pad(total, ((0, 0), (0, 0), (0, 0), (4, 4)))
    total = taps[0] * padded[:, :, :, 0:width]
    for k in range(1, 9):
        total = total + taps[k] * padded[:, :, :, k : k + width]
    return total


def shards(volumes, depth_shift, plane_shift, fraction_steps):
    sub_dev, dep_dev = (volumes.shape[0], volumes.shape[1])
    subjects = sub_dev * lax.axis_size("subj")
    padded = padded_2(volumes, (("depth", 1),), BRICK)
    warped = lax.map(
        lambda group: warp_subject(*group), (padded, depth_shift, plane_shift, fraction_steps)
    )
    local_sum = jnp.sum(warped.astype(jnp.float32), 0)
    total = lax.psum(local_sum.astype(jnp.bfloat16), "subj").astype(jnp.float32)
    template = (total / subjects).astype(jnp.bfloat16)
    stacked = jnp.concatenate([warped, template[None]], 0)
    extended = padded_2(stacked, (("depth", 1),), 2)
    templ_ext = extended[sub_dev].astype(jnp.float32)
    force = lax.map(
        lambda image: force_of(image.astype(jnp.float32), templ_ext).astype(jnp.bfloat16),
        extended[:sub_dev],
    )
    force_ext = padded_2(force, (("depth", 2),), 4)
    velocity = lax.map(
        lambda field: (8.0 * smooth(field.astype(jnp.float32))).astype(jnp.bfloat16), force_ext
    )
    return (velocity, template)


def solution(mesh):
    return jax.shard_map(
        shards,
        mesh=mesh,
        in_specs=(
            P("subj", "depth", None, None),
            P("subj", "depth"),
            P("subj", "depth", None),
            P("subj", "depth", None),
        ),
        out_specs=(P("subj", None, "depth", None, None), P("depth", None, None)),
        check_vma=False,
    )
```

profile of v0, /device:TPU:8, one launch (start us, length us, event | category | flops | bytes accessed | tf_op | source)
XLA Modules:
  0.0 274.6 jit_solution(13350816660858477998)
XLA Ops:
  7.2 3.4 %collective-permute-start = (bf16[1,8,256,256]{3,2,1,0:T(8,128)(2,1)}, bf16[1,8,256,256]{3,2,1,0:T(8,128)(2,1)S(1)}, u32[]{:S(2)}, u32[]{:S(2)}) collective-permute-start(bf16[1,8,256,256]{3,2,1,0:T(8,128)(2,1)} %param.4), channel_id=1, source_target_pairs={{0,1},{1,2},{2,3},{3,4},{4,5},{5,6},{6,7},{7,8},{8,9},{9,10},{10,1... | collective-permute-start | bytes 3145736 | tf_op jit(solution)/shard_map/ppermute | solution.py:23
  10.6 5.5 %collective-permute-start.1 = (bf16[1,8,256,256]{3,2,1,0:T(8,128)(2,1)}, bf16[1,8,256,256]{3,2,1,0:T(8,128)(2,1)S(1)}, u32[]{:S(2)}, u32[]{:S(2)}) collective-permute-start(bf16[1,8,256,256]{3,2,1,0:T(8,128)(2,1)} %param.4), channel_id=1, source_target_pairs={{1,0},{2,1},{3,2},{4,3},{5,4},{6,5},{7,6},{8,7},{9,8},{10,9},{11,1... | collective-permute-start | bytes 3145736 | tf_op jit(solution)/shard_map/ppermute | solution.py:25
  23.8 13.5 %collective-permute-done = bf16[1,8,256,256]{3,2,1,0:T(8,128)(2,1)S(1)} collective-permute-done((bf16[1,8,256,256]{3,2,1,0:T(8,128)(2,1)}, bf16[1,8,256,256]{3,2,1,0:T(8,128)(2,1)S(1)}, u32[]{:S(2)}, u32[]{:S(2)}) %collective-permute-start) | collective-permute-done | bytes 1048608 | tf_op jit(solution)/shard_map/ppermute | solution.py:23
  38.5 1.8 fusion.92
  42.3 3.0 %fusion.101 = bf16[8,256,256]{2,1,0:T(8,128)(2,1)} fusion(f32[]{:T(128)} %bitcast.16, s32[]{:T(128)S(6)} %add.581, f32[]{:T(128)} %bitcast.15, s32[]{:T(128)} %bitcast.14, f32[1,8,256,256]{3,2,1,0:T(8,128)S(1)} %fusion.85), kind=kLoop, calls=%fused_computation.194 | loop fusion | flops 2097152 | bytes 3145744 | tf_op jit(solution)/shard_map/convert_element_type | solution.py:128
  45.2 2.0 fusion.35
  47.2 46.8 %all-reduce.20.cloned.1.call-done = bf16[8,256,256]{2,1,0:T(8,128)(2,1)} async-done(((bf16[8,256,256]{2,1,0:T(8,128)(2,1)}), bf16[8,256,256]{2,1,0:T(8,128)(2,1)}) %all-reduce.20.cloned.1.call-update) | async-done | bytes 1048592 | tf_op jit(solution)/shard_map/psum | solution.py:128
  95.5 4.7 %collective-permute-start.3 = (bf16[2,2,256,256]{3,2,1,0:T(8,128)(2,1)S(1)}, bf16[2,2,256,256]{3,2,1,0:T(8,128)(2,1)S(1)}, u32[]{:S(2)}, u32[]{:S(2)}) collective-permute-start(bf16[2,2,256,256]{3,2,1,0:T(8,128)(2,1)S(1)} %get-tuple-element.86), channel_id=1, source_target_pairs={{1,0},{2,1},{3,2},{4,3},{5,4},{6,5},{7,6},{8,7},{9,8},{10,9},{11,1... | collective-permute-start | bytes 1572872 | tf_op jit(solution)/shard_map/ppermute | solution.py:25
  100.2 2.1 collective-permute-start.2
  102.3 9.6 %collective-permute-done.3 = bf16[2,2,256,256]{3,2,1,0:T(8,128)(2,1)S(1)} collective-permute-done((bf16[2,2,256,256]{3,2,1,0:T(8,128)(2,1)S(1)}, bf16[2,2,256,256]{3,2,1,0:T(8,128)(2,1)S(1)}, u32[]{:S(2)}, u32[]{:S(2)}) %collective-permute-start.3) | collective-permute-done | bytes 524320 | tf_op jit(solution)/shard_map/ppermute | solution.py:25
  111.9 7.1 %collective-permute-done.2 = bf16[2,2,256,256]{3,2,1,0:T(8,128)(2,1)S(1)} collective-permute-done((bf16[2,2,256,256]{3,2,1,0:T(8,128)(2,1)S(1)}, bf16[2,2,256,256]{3,2,1,0:T(8,128)(2,1)S(1)}, u32[]{:S(2)}, u32[]{:S(2)}) %collective-permute-start.2) | collective-permute-done | bytes 524320 | tf_op jit(solution)/shard_map/ppermute | solution.py:23
  121.4 1.4 fusion.74
  123.6 2.1 slice_add_fusion.14
  127.3 2.2 slice_add_fusion.15
  129.5 2.1 slice_add_fusion.16
  131.9 2.2 slice_add_fusion.17
  134.1 23.8 %fusion.93 = (bf16[1,1,8,256,256]{4,3,2,1,0:T(8,128)(2,1)S(1)}, f32[8,256,256]{2,1,0:T(8,128)S(1)}) fusion(f32[1,12,256,256]{3,2,1,0:T(8,128)S(1)} %get-tuple-element.84, f32[1,12,256,256]{3,2,1,0:T(8,128)S(1)} %get-tuple-element.83, f32[8,256,256]{2,1,0:T(8,128)S(1)} %slice_add_fusion.13, f32[8,256,256]{2,1,0:T(8,128)} %slice_add_fusion.14, ...), kind=kLoop, calls=%fused_computation.184 | loop fusion | flops 24117248 | bytes 22020096 | tf_op jit(solution)/shard_map/while/body/eval_jaxpr/stack | solution.py:93
  159.8 1.9 collective-permute-start.5
  161.7 3.9 %collective-permute-start.4 = (bf16[1,3,4,256,256]{4,3,2,1,0:T(8,128)(2,1)S(1)}, bf16[1,3,4,256,256]{4,3,2,1,0:T(8,128)(2,1)S(1)}, u32[]{:S(2)}, u32[]{:S(2)}) collective-permute-start(bf16[1,3,4,256,256]{4,3,2,1,0:T(8,128)(2,1)S(1)} %get-tuple-element.78), channel_id=1, source_target_pairs={{0,1},{1,2},{2,3},{3,4},{4,5},{5,6},{6,7},{7,8},{8,9},{9,10},{10,1... | collective-permute-start | bytes 4718600 | tf_op jit(solution)/shard_map/ppermute | solution.py:23
  166.9 30.4 %collective-permute-done.5 = bf16[1,3,4,256,256]{4,3,2,1,0:T(8,128)(2,1)S(1)} collective-permute-done((bf16[1,3,4,256,256]{4,3,2,1,0:T(8,128)(2,1)S(1)}, bf16[1,3,4,256,256]{4,3,2,1,0:T(8,128)(2,1)S(1)}, u32[]{:S(2)}, u32[]{:S(2)}) %collective-permute-start.5) | collective-permute-done | bytes 1572896 | tf_op jit(solution)/shard_map/ppermute | solution.py:25
  197.2 4.9 %collective-permute-done.4 = bf16[1,3,4,256,256]{4,3,2,1,0:T(8,128)(2,1)S(1)} collective-permute-done((bf16[1,3,4,256,256]{4,3,2,1,0:T(8,128)(2,1)S(1)}, bf16[1,3,4,256,256]{4,3,2,1,0:T(8,128)(2,1)S(1)}, u32[]{:S(2)}, u32[]{:S(2)}) %collective-permute-start.4) | collective-permute-done | bytes 1572896 | tf_op jit(solution)/shard_map/ppermute | solution.py:23
  203.3 6.3 %fusion.18 = f32[3,8,256,256]{3,2,1,0:T(8,128)} fusion(f32[3,16,256,256]{3,2,1,0:T(8,128)S(1)} %fusion.26), kind=kLoop, calls=%fused_computation.27 | loop fusion | flops 26738688 | bytes 62914560 | tf_op jit(solution)/shard_map/while/body/eval_jaxpr/add | solution.py:108
  209.6 27.2 %multiply_add_fusion = f32[3,8,256,256]{3,2,1,0:T(8,128)} fusion(f32[3,8,256,256]{3,2,1,0:T(8,128)} %fusion.18), kind=kLoop, calls=%fused_computation.45 | loop fusion | flops 26738688 | bytes 12582912 | tf_op jit(solution)/shard_map/while/body/eval_jaxpr/add | solution.py:112
  236.8 31.0 %fusion.32 = bf16[1,3,8,256,256]{4,3,2,1,0:T(8,128)(2,1)} fusion(f32[3,8,256,256]{3,2,1,0:T(8,128)} %multiply_add_fusion), kind=kLoop, calls=%fused_computation.83 | loop fusion | flops 29884416 | bytes 9437184 | tf_op jit(solution)/shard_map/while/body/jit(dynamic_update_index_in_dim)/broadcast_in_dim | solution.py:133
  (24 shorter events, 16.7 us)
Async XLA Ops:
  7.2 86.8 %all-reduce.20.cloned.1.call-start = ((), (), s32[]{:S(2)}) async-start(), calls=%async_computation | async-start | bytes 2097152 | tf_op jit(solution)/shard_map/psum | solution.py:128
  7.2 30.0 %collective-permute-start = (bf16[1,8,256,256]{3,2,1,0:T(8,128)(2,1)}, bf16[1,8,256,256]{3,2,1,0:T(8,128)(2,1)S(1)}, u32[]{:S(2)}, u32[]{:S(2)}) collective-permute-start(bf16[1,8,256,256]{3,2,1,0:T(8,128)(2,1)} %param.4), channel_id=1, source_target_pairs={{0,1},{1,2},{2,3},{3,4},{4,5},{5,6},{6,7},{7,8},{8,9},{9,10},{10,1... | collective-permute-start | bytes 3145736 | tf_op jit(solution)/shard_map/ppermute | solution.py:23
  10.6 27.9 %collective-permute-start.1 = (bf16[1,8,256,256]{3,2,1,0:T(8,128)(2,1)}, bf16[1,8,256,256]{3,2,1,0:T(8,128)(2,1)S(1)}, u32[]{:S(2)}, u32[]{:S(2)}) collective-permute-start(bf16[1,8,256,256]{3,2,1,0:T(8,128)(2,1)} %param.4), channel_id=1, source_target_pairs={{1,0},{2,1},{3,2},{4,3},{5,4},{6,5},{7,6},{8,7},{9,8},{10,9},{11,1... | collective-permute-start | bytes 3145736 | tf_op jit(solution)/shard_map/ppermute | solution.py:25
  95.5 16.3 %collective-permute-start.3 = (bf16[2,2,256,256]{3,2,1,0:T(8,128)(2,1)S(1)}, bf16[2,2,256,256]{3,2,1,0:T(8,128)(2,1)S(1)}, u32[]{:S(2)}, u32[]{:S(2)}) collective-permute-start(bf16[2,2,256,256]{3,2,1,0:T(8,128)(2,1)S(1)} %get-tuple-element.86), channel_id=1, source_target_pairs={{1,0},{2,1},{3,2},{4,3},{5,4},{6,5},{7,6},{8,7},{9,8},{10,9},{11,1... | collective-permute-start | bytes 1572872 | tf_op jit(solution)/shard_map/ppermute | solution.py:25
  100.2 18.8 %collective-permute-start.2 = (bf16[2,2,256,256]{3,2,1,0:T(8,128)(2,1)S(1)}, bf16[2,2,256,256]{3,2,1,0:T(8,128)(2,1)S(1)}, u32[]{:S(2)}, u32[]{:S(2)}) collective-permute-start(bf16[2,2,256,256]{3,2,1,0:T(8,128)(2,1)S(1)} %get-tuple-element.85), channel_id=1, source_target_pairs={{0,1},{1,2},{2,3},{3,4},{4,5},{5,6},{6,7},{7,8},{8,9},{9,10},{10,1... | collective-permute-start | bytes 1572872 | tf_op jit(solution)/shard_map/ppermute | solution.py:23
  159.5 6.2 %copy-start = (bf16[8,256,256]{2,1,0:T(8,128)(2,1)S(1)}, bf16[8,256,256]{2,1,0:T(8,128)(2,1)}, u32[]{:S(2)}) copy-start(bf16[8,256,256]{2,1,0:T(8,128)(2,1)} %all-reduce.20.cloned.1.call-done) | copy-start | bytes 3145732
  159.8 37.4 %collective-permute-start.5 = (bf16[1,3,4,256,256]{4,3,2,1,0:T(8,128)(2,1)S(1)}, bf16[1,3,4,256,256]{4,3,2,1,0:T(8,128)(2,1)S(1)}, u32[]{:S(2)}, u32[]{:S(2)}) collective-permute-start(bf16[1,3,4,256,256]{4,3,2,1,0:T(8,128)(2,1)S(1)} %get-tuple-element.79), channel_id=1, source_target_pairs={{1,0},{2,1},{3,2},{4,3},{5,4},{6,5},{7,6},{8,7},{9,8},{10,9},{11,1... | collective-permute-start | bytes 4718600 | tf_op jit(solution)/shard_map/ppermute | solution.py:25
  161.7 40.4 %collective-permute-start.4 = (bf16[1,3,4,256,256]{4,3,2,1,0:T(8,128)(2,1)S(1)}, bf16[1,3,4,256,256]{4,3,2,1,0:T(8,128)(2,1)S(1)}, u32[]{:S(2)}, u32[]{:S(2)}) collective-permute-start(bf16[1,3,4,256,256]{4,3,2,1,0:T(8,128)(2,1)S(1)} %get-tuple-element.78), channel_id=1, source_target_pairs={{0,1},{1,2},{2,3},{3,4},{4,5},{5,6},{6,7},{7,8},{8,9},{9,10},{10,1... | collective-permute-start | bytes 4718600 | tf_op jit(solution)/shard_map/ppermute | solution.py:23
Sparse Core Ops, SparseCore 0:
  45.4 48.5 all-reduce.19
where the time goes:
time: 275 us
  other arithmetic  118 us (43%)
  waiting for transfers between devices  114 us (41%)
  starting transfers between devices  21.5 us (8%)
  between operations  19.3 us (7%)
    psum x1, waiting for transfers between devices, shards(): total = lax.psum(local_sum.astype(jnp.bfloat16), 'subj').astype(jnp.float32)  46.8 us
    ppermute x3, waiting for transfers between devices, padded_2(): lax.ppermute(head, axis, [((i + 1) % count, i) for i in range(ends)])  41.2 us
    broadcast_in_dim x1, other arithmetic, shards(): lax.map(lambda image: force_of(image.astype(jnp.float32), templ_ext).asty...  31 us
    add x1, other arithmetic, smooth(): total = total + taps[k] * padded[:, :, k:k + height]  27.2 us
    ppermute x3, waiting for transfers between devices, padded_2(): lax.ppermute(tail, axis, [(i, (i + 1) % count) for i in range(ends)])  25.5 us
    another operation x3, other arithmetic, force_of(): return jnp.stack([common * grad_z, common * grad_y, common * grad_x])  25.4 us
    ppermute x3, starting transfers between devices, padded_2(): lax.ppermute(head, axis, [((i + 1) % count, i) for i in range(ends)])  12 us
    ppermute x3, starting transfers between devices, padded_2(): lax.ppermute(tail, axis, [(i, (i + 1) % count) for i in range(ends)])  9.42 us
  transfers between devices with their start and end apart: 7, of which 7 were waited for; matrix products, arithmetic and copies ran while one was open for 2% of the time, Pallas kernels for 0%

commit v1 on v0

v1 whole, which is shorter than its diff:
```python
import math

import jax
import jax.numpy as jnp
from jax import lax
from jax.experimental import pallas as pl
from jax.experimental.pallas import tpu as pltpu
from jax.sharding import PartitionSpec as P

MESH = pl.DeviceIdType.MESH
F32, BF16 = jnp.float32, jnp.bfloat16
H = W = 256
B = 8
HALO = 6
NE = B + 2 * HALO
PAD = 16
EPS = 1e-5
SRC = (0, 64, 128, 192, 256)
C = len(SRC) - 1


def lagging(ends):
    return tuple(max(e - 16, 0) if e < H else H for e in ends)


WE = lagging(SRC)
FE = lagging(WE)
GE = lagging(FE)
NF = max(FE[i + 1] - FE[i] for i in range(C))
G = 16

SRC_R, SRC_L, W_R, W_L, W_C, S_Z, T_C, T_R, T_L, R_L, R_R = range(11)


def taps():
    raw = [math.exp(-(t * t) / 4.5) for t in range(-4, 5)]
    total = sum(raw)
    return [r / total for r in raw]


def iota(shape, dim):
    return lax.broadcasted_iota(jnp.int32, shape, dim)


def gauss_matrix(rows, cols, shift):
    away = jnp.abs(iota((rows, cols), 0) + shift - iota((rows, cols), 1))
    w = taps()
    out = jnp.zeros((rows, cols), F32)
    for t in range(5):
        out = jnp.where(away == t, F32(w[4 + t]), out)
    return out.astype(BF16)


def dot(a, b):
    return jnp.dot(a, b, preferred_element_type=F32)


def rounded_gain():
    import numpy as np
    import ml_dtypes
    w = np.array(taps(), np.float32)
    return float(w.sum()) / float(w.astype(ml_dtypes.bfloat16).astype(np.float32).sum())


def kernel(vol, dsh, psh, fst, vel, tmpl, *refs):
    ext = refs[:C]
    (iext, text, wp, sb, sz, yb, gy, sp, bq, fo, zs, vst, ax2, bx3, dx, gx, ssem, rsem, lsem) = refs[C:]
    me, d = lax.axis_index("subj"), lax.axis_index("depth")
    nd = lax.axis_size("depth")
    core = lax.rem(me, 2)
    mate = me + 1 - 2 * core
    far = lax.rem(me + 2, 4)
    right, left = lax.rem(d + 1, nd), lax.rem(d + nd - 1, nd)
    has_l, has_r = d > 0, d < nd - 1

    def remote(src, dst, p, kind, subj, depth):
        return pltpu.make_async_remote_copy(
            src_ref=src, dst_ref=dst, send_sem=ssem.at[p, kind], recv_sem=rsem.at[p, kind],
            device_id={"subj": subj, "depth": depth}, device_id_type=MESH)

    barrier = pltpu.get_barrier_semaphore()

    def greet(subj, depth):
        pl.semaphore_signal(barrier, inc=1, device_id={"subj": subj, "depth": depth}, device_id_type=MESH)

    greet(mate, d)
    greet(far, d)

    @pl.when(has_l)
    def _():
        greet(me, left)

    @pl.when(has_r)
    def _():
        greet(me, right)

    mine = pl.ds(pl.multiple_of(core * 128, 128), 128)
    other = pl.ds(pl.multiple_of((1 - core) * 128, 128), 128)

    def rows_of(ends, p):
        return pl.ds(ends[p], ends[p + 1] - ends[p])

    def padded_rows(ends, p):
        return pl.ds(PAD + ends[p], ends[p + 1] - ends[p])

    def copy_of(p, kind):
        if kind == SRC_R:
            return remote(vol.at[:, rows_of(SRC, p), :], ext[p].at[0:B], p, kind, me, right)
        if kind == SRC_L:
            return remote(vol.at[:, rows_of(SRC, p), :], ext[p].at[2 * B:3 * B], p, kind, me, left)
        r, q = rows_of(WE, p), padded_rows(WE, p)
        if kind == W_R:
            return remote(iext.at[B:B + HALO, q, :], iext.at[0:HALO, q, :], p, kind, me, right)
        if kind == W_L:
            return remote(iext.at[HALO:2 * HALO, q, :], iext.at[B + HALO:NE, q, :], p, kind, me, left)
        if kind == W_C:
            return remote(iext.at[HALO:HALO + B, q, other], wp.at[:, r, :], p, kind, mate, d)
        if kind == S_Z:
            return remote(sb.at[:, r, :], sz.at[:, r, :], p, kind, far, d)
        if kind == T_C:
            part = text.at[HALO:HALO + B, q, mine]
            return remote(part, part, p, kind, mate, d)
        if kind == T_R:
            return remote(text.at[B:B + HALO, q, mine], text.at[0:HALO, q, mine], p, kind, me, right)
        if kind == T_L:
            return remote(text.at[HALO:2 * HALO, q, mine], text.at[B + HALO:NE, q, mine], p, kind, me, left)
        part = text.at[0:HALO, q, mine] if kind == R_L else text.at[B + HALO:NE, q, mine]
        return remote(part, part, p, kind, mate, d)

    sends = {SRC_R: has_r, W_R: has_r, T_R: has_r, SRC_L: has_l, W_L: has_l, T_L: has_l, R_L: has_l, R_R: has_r}
    gets = {SRC_R: has_l, W_R: has_l, T_R: has_l, SRC_L: has_r, W_L: has_r, T_L: has_r, R_L: has_l, R_R: has_r}

    def start(p, *kinds):
        for kind in kinds:
            if kind in sends:
                pl.when(sends[kind])(lambda kind=kind: copy_of(p, kind).start())
            else:
                copy_of(p, kind).start()

    def landed(p, *kinds):
        for kind in kinds:
            if kind in gets:
                pl.when(gets[kind])(lambda kind=kind: copy_of(p, kind).wait_recv())
            else:
                copy_of(p, kind).wait_recv()

    def own_copy(p):
        return pltpu.make_async_copy(vol.at[:, rows_of(SRC, p), :], ext[p].at[B:2 * B], lsem.at[p])

    for p in range(C):
        own_copy(p).start()

    pl.semaphore_wait(barrier, 2 + has_l.astype(jnp.int32) + has_r.astype(jnp.int32))
    for p in range(C):
        start(p, SRC_R, SRC_L)

    dz, dy, dxs = dsh[0], psh[0], psh[1]
    fz, fy, fx = fst[0].astype(F32) * 0.25, fst[1].astype(F32) * 0.25, fst[2].astype(F32) * 0.25

    def zero_pads(ref, count):
        zero = jnp.zeros((PAD, W), BF16)

        def body(z, carry):
            ref[z, 0:PAD, :] = zero
            ref[z, PAD + H:2 * PAD + H, :] = zero
            return carry
        lax.fori_loop(0, count, body, 0)

    zero_pads(iext, NE)
    zero_pads(text, NE)
    for k in range(3):
        zero_pads(zs.at[k], B)

    def zero_planes(lo):
        def body(z, carry):
            zero = jnp.zeros((H, W), BF16)
            iext[lo + z, PAD:PAD + H, :] = zero
            text[lo + z, PAD:PAD + H, :] = zero
            return carry
        lax.fori_loop(0, HALO, body, 0)

    @pl.when(d == 0)
    def _():
        zero_planes(0)
        for p in range(C):
            ext[p][0:B] = jnp.zeros((B,) + ext[p].shape[1:], BF16)

    @pl.when(d == nd - 1)
    def _():
        zero_planes(B + HALO)
        for p in range(C):
            ext[p][2 * B:3 * B] = jnp.zeros((B,) + ext[p].shape[1:], BF16)

    row, col = iota((W, W), 0), iota((W, W), 1)
    a_x = jnp.where(row == col + dxs, 1.0 - fx, jnp.where(row == col + dxs + 1, fx, 0.0)).astype(BF16)
    ax2[0:W, :] = a_x
    ax2[W:2 * W, :] = a_x
    b_x = jnp.where(jnp.abs(row - col) <= 2, 1.0, 0.0).astype(BF16)
    for i in range(3):
        bx3[i * W:(i + 1) * W, :] = b_x
    dx[...] = jnp.where(row == col + 1, 0.5, jnp.where(row == col - 1, -0.5, 0.0)).astype(BF16)
    gx[...] = gauss_matrix(W, W, 0)

    def warp(p):
        a, n = WE[p], WE[p + 1] - WE[p]
        ka = 0 if p == 0 else SRC[p] - 32
        k = SRC[p + 1] - ka
        at, j = iota((n, 2 * k), 0) + (a + dy), iota((n, 2 * k), 1)
        w_z = jnp.where(j < k, 1.0 - fz, fz)
        j = jnp.where(j < k, j, j - k) + ka
        a_y = (w_z * jnp.where(j == at, 1.0 - fy, jnp.where(j == at + 1, fy, 0.0))).astype(BF16)

        def body(z, carry):
            parts = []
            for c in range(2):
                if p > 0:
                    size = SRC[p] - SRC[p - 1]
                    parts.append(ext[p - 1][8 + dz + z + c, size - 32:size, :])
                parts.append(ext[p][8 + dz + z + c])
            r = dot(a_y, jnp.concatenate(parts, 0))
            hi = r.astype(BF16)
            lo = (r - hi.astype(F32)).astype(BF16)
            out = dot(jnp.concatenate([hi, lo], 1), ax2[...])
            iext[HALO + z, PAD + a:PAD + a + n, :] = out.astype(BF16)
            return carry
        lax.fori_loop(0, B, body, 0)

    def partial_sum(p):
        r, q = rows_of(WE, p), padded_rows(WE, p)

        def body(z, carry):
            sb[z, r, :] = (iext[HALO + z, q, mine].astype(F32) + wp[z, r, :].astype(F32)).astype(BF16)
            return carry
        lax.fori_loop(0, B, body, 0)

    def template(p):
        r, q = rows_of(WE, p), padded_rows(WE, p)

        def body(z, carry):
            text[HALO + z, q, mine] = ((sb[z, r, :].astype(F32) + sz[z, r, :].astype(F32)) * 0.25).astype(BF16)
            return carry
        lax.fori_loop(0, B, body, 0)

    def force(p):
        a, n = FE[p], FE[p + 1] - FE[p]
        k = n + 2 * PAD
        away = iota((n, k), 0) + PAD - iota((n, k), 1)
        b_y = jnp.where(jnp.abs(away) <= 2, 1.0, 0.0).astype(BF16)
        d_y = jnp.where(away == -1, 0.5, jnp.where(away == 1, -0.5, 0.0)).astype(BF16)
        bd = jnp.concatenate([b_y, d_y], 0)
        b2 = jnp.concatenate([b_y, b_y], 1)

        def in_rows(z, carry):
            i, j = iext[z, a:a + k, :], text[z, a:a + k, :]
            both = dot(bd, i)
            yb[0, z, 0:n, :] = both[:n]
            gy[z, 0:n, :] = both[n:]
            yb[1, z, 0:n, :] = dot(b_y, j)
            fi, fj = i.astype(F32), j.astype(F32)
            for q, v in ((2, fi * fj), (3, fi * fi), (4, fj * fj)):
                hi = v.astype(BF16)
                lo = (v - hi.astype(F32)).astype(BF16)
                yb[q, z, 0:n, :] = dot(b2, jnp.concatenate([hi, lo], 0))
            return carry
        lax.fori_loop(0, NE, in_rows, 0)

        def plane(z, carry):
            for g in range(0, n, G):
                for q in range(5):
                    s = yb[q, z, g:g + G, :]
                    for t in range(1, 5):
                        s = s + yb[q, z + t, g:g + G, :]
                    for part in range(3):
                        piece = s.astype(BF16)
                        sp[q * n + g:q * n + g + G, part * W:(part + 1) * W] = piece
                        s = s - piece.astype(F32)
            bq[0:5 * n, :] = dot(sp[0:5 * n, :], bx3[...])
            whole = (d * B - 4 + z >= 0) & (d * B - 4 + z < nd * B)
            g_x = dot(iext[z + 2, PAD + a:PAD + a + n, :], dx[...])
            for g in range(0, n, G):
                here = slice(PAD + a + g, PAD + a + g + G)
                m_i, m_j = bq[g:g + G, :] * (1 / 125), bq[n + g:n + g + G, :] * (1 / 125)
                cov = bq[2 * n + g:2 * n + g + G, :] * (1 / 125) - m_i * m_j
                v_i = bq[3 * n + g:3 * n + g + G, :] * (1 / 125) - m_i * m_i + EPS
                v_j = bq[4 * n + g:4 * n + g + G, :] * (1 / 125) - m_j * m_j + EPS
                scaled = cov / (v_i * v_j)
                i, j = iext[z + 2, here, :].astype(F32), text[z + 2, here, :].astype(F32)
                common = 2.0 * scaled * ((j - m_j) - scaled * v_j * (i - m_i))
                common = jnp.where(whole, common, 0.0)
                g_z = (iext[z + 3, here, :].astype(F32) - iext[z + 1, here, :].astype(F32)) * 0.5
                fo[0, z, g:g + G, :] = (common * g_z).astype(BF16)
                fo[1, z, g:g + G, :] = (common * gy[z + 2, g:g + G, :]).astype(BF16)
                fo[2, z, g:g + G, :] = (common * g_x[g:g + G]).astype(BF16)
            return carry
        lax.fori_loop(0, 2 * B, plane, 0)

        w = [8.0 * rounded_gain() ** 2 * t for t in taps()]

        def along_depth(g, carry):
            r = pl.ds(pl.multiple_of(g * G, G), G)
            out = pl.ds(pl.multiple_of(PAD + a + g * G, G), G)
            for k3 in range(3):
                for half in range(2):
                    lanes = slice(half * 128, half * 128 + 128)
                    f = [fo[k3, z, r, lanes].astype(F32) for z in range(2 * B)]
                    for z in range(B):
                        s = f[z + 4] * w[4]
                        for t in range(1, 5):
                            s = s + (f[z + 4 - t] + f[z + 4 + t]) * w[4 + t]
                        zs[k3, z, out, lanes] = s.astype(BF16)
            return carry
        lax.fori_loop(0, n // G, along_depth, 0)

    def out_copy(p):
        r = rows_of(GE, p)
        return pltpu.make_async_copy(vst.at[:, :, r, :], vel.at[:, :, r, :], lsem.at[C + p])

    def smooth(p):
        a, n = GE[p], GE[p + 1] - GE[p]
        if n == 0:
            return
        g_y = gauss_matrix(n, n + 2 * PAD, PAD)

        def body(z, carry):
            for k3 in range(3):
                r = dot(g_y, zs[k3, z, a:a + n + 2 * PAD, :]).astype(BF16)
                vst[k3, z, a:a + n, :] = dot(r, gx[...]).astype(BF16)
            return carry
        lax.fori_loop(0, B, body, 0)
        out_copy(p).start()

    for t in range(C + 3):
        if t < C:
            own_copy(t).wait()
            landed(t, SRC_R, SRC_L)
            warp(t)
            start(t, W_C, W_R, W_L)
            landed(t, W_C)
            partial_sum(t)
            start(t, S_Z)
        p = t - 1
        if 0 <= p < C:
            landed(p, S_Z)
            template(p)
            start(p, T_R, T_L, T_C)
        p = t - 2
        if 0 <= p < C:
            landed(p, T_R, T_L)
            start(p, R_L, R_R)
        p = t - 3
        if 0 <= p < C:
            landed(p, W_R, W_L, T_C, R_L, R_R)
            if p == C - 1:
                whole_template = pltpu.make_async_copy(
                    text.at[HALO:HALO + B, PAD:PAD + H, :], tmpl, lsem.at[2 * C])
                whole_template.start()
            force(p)
            smooth(p)

    for p in range(C):
        if GE[p + 1] > GE[p]:
            out_copy(p).wait()
    whole_template.wait()
    for p in range(C):
        for kind in range(11):
            if kind in sends:
                pl.when(sends[kind])(lambda kind=kind: copy_of(p, kind).wait_send())
            else:
                copy_of(p, kind).wait_send()


def shards(volumes, depth_shift, plane_shift, fraction_steps):
    smem = pl.BlockSpec(memory_space=pltpu.SMEM)
    anywhere = pl.BlockSpec(memory_space=pl.ANY)
    scratch = [pltpu.VMEM((3 * B, SRC[p + 1] - SRC[p], W), BF16) for p in range(C)]
    scratch += [
        pltpu.VMEM((NE, H + 2 * PAD, W), BF16),
        pltpu.VMEM((NE, H + 2 * PAD, W), BF16),
        pltpu.VMEM((B, H, 128), BF16),
        pltpu.VMEM((B, H, 128), BF16),
        pltpu.VMEM((B, H, 128), BF16),
        pltpu.VMEM((5, NE, NF, W), F32),
        pltpu.VMEM((NE, NF, W), F32),
        pltpu.VMEM((5 * NF, 3 * W), BF16),
        pltpu.VMEM((5 * NF, W), F32),
        pltpu.VMEM((3, 2 * B, NF, W), BF16),
        pltpu.VMEM((3, B, H + 2 * PAD, W), BF16),
        pltpu.VMEM((3, B, H, W), BF16),
        pltpu.VMEM((2 * W, W), BF16),
        pltpu.VMEM((3 * W, W), BF16),
        pltpu.VMEM((W, W), BF16),
        pltpu.VMEM((W, W), BF16),
        pltpu.SemaphoreType.DMA((C, 11)),
        pltpu.SemaphoreType.DMA((C, 11)),
        pltpu.SemaphoreType.DMA((2 * C + 1,)),
    ]
    velocity, template = pl.pallas_call(
        kernel,
        out_shape=(jax.ShapeDtypeStruct((3, B, H, W), BF16), jax.ShapeDtypeStruct((B, H, W), BF16)),
        in_specs=[anywhere, smem, smem, smem],
        out_specs=(anywhere, anywhere),
        scratch_shapes=scratch,
        compiler_params=pltpu.CompilerParams(
            collective_id=0, has_side_effects=True, vmem_limit_bytes=56 * 1024 * 1024),
    )(volumes[0], depth_shift.reshape(1), plane_shift.reshape(2), fraction_steps.reshape(3))
    return velocity[None], template


def solution(mesh):
    return jax.shard_map(
        shards,
        mesh=mesh,
        in_specs=(
            P("subj", "depth", None, None),
            P("subj", "depth"),
            P("subj", "depth", None),
            P("subj", "depth", None),
        ),
        out_specs=(P("subj", None, "depth", None, None), P("depth", None, None)),
        check_vma=False,
    )
```

time: 275 us -> 129 us (0.47)
  Pallas kernels: 0 us -> 122 us
  other arithmetic: 118 us -> 0 us
  waiting for transfers between devices: 114 us -> 0 us
  starting transfers between devices: 21.5 us -> 0 us
  between operations: 19.3 us -> 1.29 us
    pallas_call x0 -> x1, Pallas kernels: none -> 122 us  [shards(): pl.pallas_call(kernel, out_shape=(jax.ShapeDtypeStruct((3, B, H, W), BF16...]
    ppermute x6 -> x0, waiting for transfers between devices: 66.7 us -> none  [the longest x3 41.2 us: padded_2(): lax.ppermute(head, axis, [((i + 1) % count, i) for i in range(ends)])]
    add x12 -> x0, other arithmetic: 48 us -> none  [the longest x1 27.2 us: smooth(): total = total + taps[k] * padded[:, :, k:k + height]]
    psum x1 -> x0, waiting for transfers between devices: 46.8 us -> none  [shards(): total = lax.psum(local_sum.astype(jnp.bfloat16), 'subj').astype(jnp.float32)]
    broadcast_in_dim x2 -> x0, other arithmetic: 32.4 us -> none  [the longest x1 31 us: shards(): lax.map(lambda image: force_of(image.astype(jnp.float32), templ_ext).asty...]
    another operation x3 -> x0, other arithmetic: 25.4 us -> none  [force_of(): return jnp.stack([common * grad_z, common * grad_y, common * grad_x])]
    ppermute x6 -> x0, starting transfers between devices: 21.5 us -> none  [the longest x3 12 us: padded_2(): lax.ppermute(head, axis, [((i + 1) % count, i) for i in range(ends)])]
    convert_element_type x6 -> x0, other arithmetic: 9.72 us -> none  [the longest x1 2.95 us: shards(): total = lax.psum(local_sum.astype(jnp.bfloat16), 'subj').astype(jnp.float32)]
  transfers between devices with their start and end apart: 7 -> 0, of which waited for: 7 -> 0; matrix products, arithmetic and copies ran while one was open for 2% -> 0% of each run, Pallas kernels for 0% -> 0%
where the time goes in v1:
time: 129 us; the launch traced here: 128 us
  Pallas kernels  122 us (95%)
  local copies, waits for them, and re-layouts  4.92 us (4%)
  between operations  1.29 us (1%)
    pallas_call x1, Pallas kernels, shards(): pl.pallas_call(kernel, out_shape=(jax.ShapeDtypeStruct((3, B, H, W), BF16...  122 us
    unnamed x4, local copies, waits for them, and re-layouts  4.92 us

profile of v1, /device:TPU:8, one launch (start us, length us, event | category | flops | bytes accessed | tf_op | source)
XLA Modules:
  0.0 128.1 jit_solution(16376877987676260418)
XLA Ops:
  1.3 121.9 %shard_map.59 = (bf16[3,8,256,256]{3,2,1,0:T(8,128)(2,1)}, bf16[8,256,256]{2,1,0:T(8,128)(2,1)}) custom-call(bf16[8,256,256]{2,1,0:T(8,128)(2,1)} %bitcast.7, s32[1]{0:T(128)} %bitcast.5.dsh, s32[2]{0:T(128)} %bitcast.8, s32[3]{0:T(128)} %bitcast.9), custom_call_target="tpu_custom_call" | custom-call | tf_op jit(solution)/shard_map/pallas_call | solution.py:397
  123.2 0.0 copy-start
  123.2 3.9 %copy.9 = bf16[1,3,8,256,256]{4,3,2,1,0:T(8,128)(2,1)} copy(bf16[1,3,8,256,256]{4,3,2,1,0:T(8,128)(2,1)} %bitcast.6) | data formatting | bytes 6291456
  127.1 0.0 copy-done
  127.1 1.0 copy.10
Async XLA Ops:
  123.2 4.0 %copy-start = (bf16[8,256,256]{2,1,0:T(8,128)(2,1)S(1)}, bf16[8,256,256]{2,1,0:T(8,128)(2,1)}, u32[]{:S(2)}) copy-start(bf16[8,256,256]{2,1,0:T(8,128)(2,1)} %get-tuple-element.9) | copy-start | bytes 3145732

commit v2 on v1

--- a/solution.py
+++ b/solution.py
@@ -28,6 +28,7 @@
 GE = lagging(FE)
 NF = max(FE[i + 1] - FE[i] for i in range(C))
 G = 16
+U = 4
 
 SRC_R, SRC_L, W_R, W_L, W_C, S_Z, T_C, T_R, T_L, R_L, R_R = range(11)
 
@@ -64,7 +65,7 @@
 
 def kernel(vol, dsh, psh, fst, vel, tmpl, *refs):
     ext = refs[:C]
-    (iext, text, wp, sb, sz, yb, gy, sp, bq, fo, zs, vst, ax2, bx3, dx, gx, ssem, rsem, lsem) = refs[C:]
+    (iext, text, wp, sb, sz, yb, gy, sp, bq, gxs, fo, zs, vst, ax2, bx3, dx, gx, ssem, rsem, lsem) = refs[C:]
     me, d = lax.axis_index("subj"), lax.axis_index("depth")
     nd = lax.axis_size("depth")
     core = lax.rem(me, 2)
@@ -210,20 +211,21 @@
         j = jnp.where(j < k, j, j - k) + ka
         a_y = (w_z * jnp.where(j == at, 1.0 - fy, jnp.where(j == at + 1, fy, 0.0))).astype(BF16)
 
-        def body(z, carry):
-            parts = []
-            for c in range(2):
-                if p > 0:
-                    size = SRC[p] - SRC[p - 1]
-                    parts.append(ext[p - 1][8 + dz + z + c, size - 32:size, :])
-                parts.append(ext[p][8 + dz + z + c])
-            r = dot(a_y, jnp.concatenate(parts, 0))
-            hi = r.astype(BF16)
-            lo = (r - hi.astype(F32)).astype(BF16)
-            out = dot(jnp.concatenate([hi, lo], 1), ax2[...])
-            iext[HALO + z, PAD + a:PAD + a + n, :] = out.astype(BF16)
-            return carry
-        lax.fori_loop(0, B, body, 0)
+        for half in range(0, B, U):
+            split = []
+            for z in range(half, half + U):
+                parts = []
+                for c in range(2):
+                    if p > 0:
+                        size = SRC[p] - SRC[p - 1]
+                        parts.append(ext[p - 1][8 + dz + z + c, size - 32:size, :])
+                    parts.append(ext[p][8 + dz + z + c])
+                r = dot(a_y, jnp.concatenate(parts, 0))
+                hi = r.astype(BF16)
+                lo = (r - hi.astype(F32)).astype(BF16)
+                split.append(jnp.concatenate([hi, lo], 1))
+            out = dot(jnp.concatenate(split, 0), ax2[...]).astype(BF16)
+            iext[HALO + half:HALO + half + U, PAD + a:PAD + a + n, :] = out.reshape(U, n, W)
 
     def partial_sum(p):
         r, q = rows_of(WE, p), padded_rows(WE, p)
@@ -250,7 +252,7 @@
         bd = jnp.concatenate([b_y, d_y], 0)
         b2 = jnp.concatenate([b_y, b_y], 1)
 
-        def in_rows(z, carry):
+        def in_rows(z):
             i, j = iext[z, a:a + k, :], text[z, a:a + k, :]
             both = dot(bd, i)
             yb[0, z, 0:n, :] = both[:n]
@@ -261,38 +263,49 @@
                 hi = v.astype(BF16)
                 lo = (v - hi.astype(F32)).astype(BF16)
                 yb[q, z, 0:n, :] = dot(b2, jnp.concatenate([hi, lo], 0))
-            return carry
-        lax.fori_loop(0, NE, in_rows, 0)
-
-        def plane(z, carry):
-            for g in range(0, n, G):
-                for q in range(5):
-                    s = yb[q, z, g:g + G, :]
-                    for t in range(1, 5):
-                        s = s + yb[q, z + t, g:g + G, :]
-                    for part in range(3):
-                        piece = s.astype(BF16)
-                        sp[q * n + g:q * n + g + G, part * W:(part + 1) * W] = piece
-                        s = s - piece.astype(F32)
-            bq[0:5 * n, :] = dot(sp[0:5 * n, :], bx3[...])
-            whole = (d * B - 4 + z >= 0) & (d * B - 4 + z < nd * B)
-            g_x = dot(iext[z + 2, PAD + a:PAD + a + n, :], dx[...])
-            for g in range(0, n, G):
-                here = slice(PAD + a + g, PAD + a + g + G)
-                m_i, m_j = bq[g:g + G, :] * (1 / 125), bq[n + g:n + g + G, :] * (1 / 125)
-                cov = bq[2 * n + g:2 * n + g + G, :] * (1 / 125) - m_i * m_j
-                v_i = bq[3 * n + g:3 * n + g + G, :] * (1 / 125) - m_i * m_i + EPS
-                v_j = bq[4 * n + g:4 * n + g + G, :] * (1 / 125) - m_j * m_j + EPS
-                scaled = cov / (v_i * v_j)
-                i, j = iext[z + 2, here, :].astype(F32), text[z + 2, here, :].astype(F32)
-                common = 2.0 * scaled * ((j - m_j) - scaled * v_j * (i - m_i))
-                common = jnp.where(whole, common, 0.0)
-                g_z = (iext[z + 3, here, :].astype(F32) - iext[z + 1, here, :].astype(F32)) * 0.5
-                fo[0, z, g:g + G, :] = (common * g_z).astype(BF16)
-                fo[1, z, g:g + G, :] = (common * gy[z + 2, g:g + G, :]).astype(BF16)
-                fo[2, z, g:g + G, :] = (common * g_x[g:g + G]).astype(BF16)
-            return carry
-        lax.fori_loop(0, 2 * B, plane, 0)
+
+        def in_rows_of(zu, carry):
+            for u in range(U):
+                in_rows(zu * U + u)
+            return carry
+        lax.fori_loop(0, NE // U, in_rows_of, 0)
+
+        def planes(zu, carry):
+            z0 = zu * U
+            for q in range(5):
+                for g in range(0, n, G):
+                    v = [yb[q, z0 + t, g:g + G, :] for t in range(8)]
+                    m12, m34, m56 = v[1] + v[2], v[3] + v[4], v[5] + v[6]
+                    low, high = m12 + m34, m34 + m56
+                    for u, s in enumerate((v[0] + low, low + v[5], v[2] + high, high + v[7])):
+                        at = (u * 5 + q) * n + g
+                        for part in range(3):
+                            piece = s.astype(BF16)
+                            sp[at:at + G, part * W:(part + 1) * W] = piece
+                            if part < 2:
+                                s = s - piece.astype(F32)
+            bq[0:5 * U * n, :] = dot(sp[0:5 * U * n, :], bx3[...])
+            gxs[0:U * n, :] = dot(iext[pl.ds(z0 + 2, U), PAD + a:PAD + a + n, :].reshape(U * n, W), dx[...])
+            for u in range(U):
+                z = z0 + u
+                whole = (d * B - 4 + z >= 0) & (d * B - 4 + z < nd * B)
+                for g in range(0, n, G):
+                    here = slice(PAD + a + g, PAD + a + g + G)
+                    b_i, b_j, b_ij, b_ii, b_jj = (
+                        bq[(u * 5 + q) * n + g:(u * 5 + q) * n + g + G, :] * (1 / 125) for q in range(5))
+                    cov = b_ij - b_i * b_j
+                    v_i = b_ii - b_i * b_i + EPS
+                    v_j = b_jj - b_j * b_j + EPS
+                    scaled = cov / (v_i * v_j)
+                    i, j = iext[z + 2, here, :].astype(F32), text[z + 2, here, :].astype(F32)
+                    common = 2.0 * scaled * ((j - b_j) - scaled * v_j * (i - b_i))
+                    common = jnp.where(whole, common, 0.0)
+                    g_z = (iext[z + 3, here, :].astype(F32) - iext[z + 1, here, :].astype(F32)) * 0.5
+                    fo[0, z, g:g + G, :] = (common * g_z).astype(BF16)
+                    fo[1, z, g:g + G, :] = (common * gy[z + 2, g:g + G, :]).astype(BF16)
+                    fo[2, z, g:g + G, :] = (common * gxs[u * n + g:u * n + g + G, :]).astype(BF16)
+            return carry
+        lax.fori_loop(0, 2 * B // U, planes, 0)
 
         w = [8.0 * rounded_gain() ** 2 * t for t in taps()]
 
@@ -321,12 +334,11 @@
             return
         g_y = gauss_matrix(n, n + 2 * PAD, PAD)
 
-        def body(z, carry):
-            for k3 in range(3):
-                r = dot(g_y, zs[k3, z, a:a + n + 2 * PAD, :]).astype(BF16)
-                vst[k3, z, a:a + n, :] = dot(r, gx[...]).astype(BF16)
-            return carry
-        lax.fori_loop(0, B, body, 0)
+        for k3 in range(3):
+            for z in range(0, B, U):
+                r = [dot(g_y, zs[k3, z + u, a:a + n + 2 * PAD, :]).astype(BF16) for u in range(U)]
+                out = dot(jnp.concatenate(r, 0), gx[...]).astype(BF16)
+                vst[k3, z:z + U, a:a + n, :] = out.reshape(U, n, W)
         out_copy(p).start()
 
     for t in range(C + 3):
@@ -381,8 +393,9 @@
         pltpu.VMEM((B, H, 128), BF16),
         pltpu.VMEM((5, NE, NF, W), F32),
         pltpu.VMEM((NE, NF, W), F32),
-        pltpu.VMEM((5 * NF, 3 * W), BF16),
-        pltpu.VMEM((5 * NF, W), F32),
+        pltpu.VMEM((5 * U * NF, 3 * W), BF16),
+        pltpu.VMEM((5 * U * NF, W), F32),
+        pltpu.VMEM((U * NF, W), F32),
         pltpu.VMEM((3, 2 * B, NF, W), BF16),
         pltpu.VMEM((3, B, H + 2 * PAD, W), BF16),
         pltpu.VMEM((3, B, H, W), BF16),

time: 129 us -> 106 us (0.82)
  Pallas kernels: 122 us -> 99.4 us
    pallas_call x1, Pallas kernels: 122 us -> 99.4 us  [shards(): pl.pallas_call(kernel, out_shape=(jax.ShapeDtypeStruct((3, B, H, W), BF16...]
where the time goes in v2:
time: 106 us
  Pallas kernels  99.4 us (94%)
  local copies, waits for them, and re-layouts  4.92 us (5%)
  between operations  1.29 us (1%)
    pallas_call x1, Pallas kernels, shards(): pl.pallas_call(kernel, out_shape=(jax.ShapeDtypeStruct((3, B, H, W), BF16...  99.4 us
    unnamed x4, local copies, waits for them, and re-layouts  4.92 us

profile of v2, /device:TPU:8, one launch (start us, length us, event | category | flops | bytes accessed | tf_op | source)
XLA Modules:
  0.0 105.6 jit_solution(5175694496968734533)
XLA Ops:
  1.3 99.4 %shard_map.59 = (bf16[3,8,256,256]{3,2,1,0:T(8,128)(2,1)}, bf16[8,256,256]{2,1,0:T(8,128)(2,1)}) custom-call(bf16[8,256,256]{2,1,0:T(8,128)(2,1)} %bitcast.7, s32[1]{0:T(128)} %bitcast.5.dsh, s32[2]{0:T(128)} %bitcast.8, s32[3]{0:T(128)} %bitcast.9), custom_call_target="tpu_custom_call" | custom-call | tf_op jit(solution)/shard_map/pallas_call | solution.py:410
  100.7 0.0 copy-start
  100.7 3.9 %copy.9 = bf16[1,3,8,256,256]{4,3,2,1,0:T(8,128)(2,1)} copy(bf16[1,3,8,256,256]{4,3,2,1,0:T(8,128)(2,1)} %bitcast.6) | data formatting | bytes 6291456
  104.6 0.0 copy-done
  104.6 1.0 copy.10
Async XLA Ops:
  100.7 4.0 %copy-start = (bf16[8,256,256]{2,1,0:T(8,128)(2,1)S(1)}, bf16[8,256,256]{2,1,0:T(8,128)(2,1)}, u32[]{:S(2)}) copy-start(bf16[8,256,256]{2,1,0:T(8,128)(2,1)} %get-tuple-element.9) | copy-start | bytes 3145732

commit v3 on v2

--- a/solution.py
+++ b/solution.py
@@ -15,7 +15,7 @@
 NE = B + 2 * HALO
 PAD = 16
 EPS = 1e-5
-SRC = (0, 64, 128, 192, 256)
+SRC = (0, 48, 96, 144, 192, 240, 256)
 C = len(SRC) - 1
 
 
@@ -341,30 +341,66 @@
                 vst[k3, z:z + U, a:a + n, :] = out.reshape(U, n, W)
         out_copy(p).start()
 
-    for t in range(C + 3):
-        if t < C:
-            own_copy(t).wait()
-            landed(t, SRC_R, SRC_L)
-            warp(t)
-            start(t, W_C, W_R, W_L)
-            landed(t, W_C)
-            partial_sum(t)
-            start(t, S_Z)
-        p = t - 1
-        if 0 <= p < C:
+    whole_template = pltpu.make_async_copy(
+        text.at[HALO:HALO + B, PAD:PAD + H, :], tmpl, lsem.at[2 * C])
+    for step, p in (
+            ('s', 0),
+            ('c', 0),
+            ('w', 0),
+            ('s', 1),
+            ('c', 1),
+            ('w', 1),
+            ('t', 0),
+            ('s', 2),
+            ('c', 2),
+            ('w', 2),
+            ('t', 1),
+            ('r', 0),
+            ('f', 0),
+            ('s', 3),
+            ('c', 3),
+            ('w', 3),
+            ('t', 2),
+            ('r', 1),
+            ('f', 1),
+            ('s', 4),
+            ('c', 4),
+            ('w', 4),
+            ('t', 3),
+            ('r', 2),
+            ('f', 2),
+            ('s', 5),
+            ('c', 5),
+            ('w', 5),
+            ('t', 4),
+            ('r', 3),
+            ('f', 3),
+            ('t', 5),
+            ('r', 4),
+            ('f', 4),
+            ('r', 5),
+            ('f', 5)):
+        if step == "s":
+            own_copy(p).wait()
+            landed(p, SRC_R, SRC_L)
+            warp(p)
+            start(p, W_C)
+        elif step == "c":
+            landed(p, W_C)
+            partial_sum(p)
+            start(p, S_Z)
+        elif step == "w":
+            start(p, W_R, W_L)
+        elif step == "t":
             landed(p, S_Z)
             template(p)
             start(p, T_R, T_L, T_C)
-        p = t - 2
-        if 0 <= p < C:
+        elif step == "r":
             landed(p, T_R, T_L)
             start(p, R_L, R_R)
-        p = t - 3
-        if 0 <= p < C:
+        elif step == "f":
             landed(p, W_R, W_L, T_C, R_L, R_R)
             if p == C - 1:
-                whole_template = pltpu.make_async_copy(
-                    text.at[HALO:HALO + B, PAD:PAD + H, :], tmpl, lsem.at[2 * C])
                 whole_template.start()
             force(p)
             smooth(p)

time: 106 us -> 101 us (0.953)
  Pallas kernels: 99.4 us -> 93.6 us
    pallas_call x1, Pallas kernels: 99.4 us -> 93.6 us  [shards(): pl.pallas_call(kernel, out_shape=(jax.ShapeDtypeStruct((3, B, H, W), BF16...]
where the time goes in v3:
time: 101 us; the launch traced here: 99.9 us
  Pallas kernels  93.6 us (93%)
  local copies, waits for them, and re-layouts  4.92 us (5%)
  between operations  1.29 us (1%)
    pallas_call x1, Pallas kernels, shards(): pl.pallas_call(kernel, out_shape=(jax.ShapeDtypeStruct((3, B, H, W), BF16...  93.6 us
    unnamed x4, local copies, waits for them, and re-layouts  4.92 us

profile of v3, /device:TPU:8, one launch (start us, length us, event | category | flops | bytes accessed | tf_op | source)
XLA Modules:
  0.0 99.9 jit_solution(6253655077460918615)
XLA Ops:
  1.3 93.6 %shard_map.59 = (bf16[3,8,256,256]{3,2,1,0:T(8,128)(2,1)}, bf16[8,256,256]{2,1,0:T(8,128)(2,1)}) custom-call(bf16[8,256,256]{2,1,0:T(8,128)(2,1)} %bitcast.7, s32[1]{0:T(128)} %bitcast.5.dsh, s32[2]{0:T(128)} %bitcast.8, s32[3]{0:T(128)} %bitcast.9), custom_call_target="tpu_custom_call" | custom-call | tf_op jit(solution)/shard_map/pallas_call | solution.py:446
  94.9 0.0 copy-start
  94.9 3.9 %copy.9 = bf16[1,3,8,256,256]{4,3,2,1,0:T(8,128)(2,1)} copy(bf16[1,3,8,256,256]{4,3,2,1,0:T(8,128)(2,1)} %bitcast.6) | data formatting | bytes 6291456
  98.9 0.0 copy-done
  98.9 1.0 copy.10
Async XLA Ops:
  94.9 4.0 %copy-start = (bf16[8,256,256]{2,1,0:T(8,128)(2,1)S(1)}, bf16[8,256,256]{2,1,0:T(8,128)(2,1)}, u32[]{:S(2)}) copy-start(bf16[8,256,256]{2,1,0:T(8,128)(2,1)} %get-tuple-element.9) | copy-start | bytes 3145732

commit v4 on v3

--- a/solution.py
+++ b/solution.py
@@ -25,10 +25,10 @@
 
 WE = lagging(SRC)
 FE = lagging(WE)
-GE = lagging(FE)
 NF = max(FE[i + 1] - FE[i] for i in range(C))
 G = 16
 U = 4
+Z = 4
 
 SRC_R, SRC_L, W_R, W_L, W_C, S_Z, T_C, T_R, T_L, R_L, R_R = range(11)
 
@@ -63,9 +63,9 @@
     return float(w.sum()) / float(w.astype(ml_dtypes.bfloat16).astype(np.float32).sum())
 
 
-def kernel(vol, dsh, psh, fst, vel, tmpl, *refs):
+def kernel(vol, dsh, psh, fst, zs_out, tmpl, *refs):
     ext = refs[:C]
-    (iext, text, wp, sb, sz, yb, gy, sp, bq, gxs, fo, zs, vst, ax2, bx3, dx, gx, ssem, rsem, lsem) = refs[C:]
+    (iext, text, wp, sb, sz, yb, gy, sp, bq, gxs, fo, zs, ax2, bx3, dx, ssem, rsem, lsem) = refs[C:]
     me, d = lax.axis_index("subj"), lax.axis_index("depth")
     nd = lax.axis_size("depth")
     core = lax.rem(me, 2)
@@ -169,8 +169,6 @@
 
     zero_pads(iext, NE)
     zero_pads(text, NE)
-    for k in range(3):
-        zero_pads(zs.at[k], B)
 
     def zero_planes(lo):
         def body(z, carry):
@@ -200,7 +198,6 @@
     for i in range(3):
         bx3[i * W:(i + 1) * W, :] = b_x
     dx[...] = jnp.where(row == col + 1, 0.5, jnp.where(row == col - 1, -0.5, 0.0)).astype(BF16)
-    gx[...] = gauss_matrix(W, W, 0)
 
     def warp(p):
         a, n = WE[p], WE[p + 1] - WE[p]
@@ -311,7 +308,7 @@
 
         def along_depth(g, carry):
             r = pl.ds(pl.multiple_of(g * G, G), G)
-            out = pl.ds(pl.multiple_of(PAD + a + g * G, G), G)
+            out = pl.ds(pl.multiple_of(a + g * G, G), G)
             for k3 in range(3):
                 for half in range(2):
                     lanes = slice(half * 128, half * 128 + 128)
@@ -325,21 +322,8 @@
         lax.fori_loop(0, n // G, along_depth, 0)
 
     def out_copy(p):
-        r = rows_of(GE, p)
-        return pltpu.make_async_copy(vst.at[:, :, r, :], vel.at[:, :, r, :], lsem.at[C + p])
-
-    def smooth(p):
-        a, n = GE[p], GE[p + 1] - GE[p]
-        if n == 0:
-            return
-        g_y = gauss_matrix(n, n + 2 * PAD, PAD)
-
-        for k3 in range(3):
-            for z in range(0, B, U):
-                r = [dot(g_y, zs[k3, z + u, a:a + n + 2 * PAD, :]).astype(BF16) for u in range(U)]
-                out = dot(jnp.concatenate(r, 0), gx[...]).astype(BF16)
-                vst[k3, z:z + U, a:a + n, :] = out.reshape(U, n, W)
-        out_copy(p).start()
+        r = rows_of(FE, p)
+        return pltpu.make_async_copy(zs.at[:, :, r, :], zs_out.at[:, :, r, :], lsem.at[C + p])
 
     whole_template = pltpu.make_async_copy(
         text.at[HALO:HALO + B, PAD:PAD + H, :], tmpl, lsem.at[2 * C])
@@ -354,29 +338,29 @@
             ('s', 2),
             ('c', 2),
             ('w', 2),
+            ('r', 0),
             ('t', 1),
-            ('r', 0),
             ('f', 0),
             ('s', 3),
             ('c', 3),
             ('w', 3),
+            ('r', 1),
             ('t', 2),
-            ('r', 1),
             ('f', 1),
             ('s', 4),
             ('c', 4),
             ('w', 4),
+            ('r', 2),
             ('t', 3),
-            ('r', 2),
             ('f', 2),
             ('s', 5),
             ('c', 5),
             ('w', 5),
+            ('r', 3),
             ('t', 4),
-            ('r', 3),
             ('f', 3),
+            ('r', 4),
             ('t', 5),
-            ('r', 4),
             ('f', 4),
             ('r', 5),
             ('f', 5)):
@@ -403,11 +387,10 @@
             if p == C - 1:
                 whole_template.start()
             force(p)
-            smooth(p)
+            out_copy(p).start()
 
     for p in range(C):
-        if GE[p + 1] > GE[p]:
-            out_copy(p).wait()
+        out_copy(p).wait()
     whole_template.wait()
     for p in range(C):
         for kind in range(11):
@@ -415,6 +398,17 @@
                 pl.when(sends[kind])(lambda kind=kind: copy_of(p, kind).wait_send())
             else:
                 copy_of(p, kind).wait_send()
+
+
+def smooth_in_plane(along, averaged, velocity, template, g):
+    @pl.when(pl.program_id(0) == 0)
+    def _():
+        g[...] = gauss_matrix(W, W, 0)
+
+    r = [dot(g[...], along[k3, z]).astype(BF16) for k3 in range(3) for z in range(Z)]
+    out = dot(jnp.concatenate(r, 0), g[...]).astype(BF16)
+    velocity[...] = out.reshape(3, Z, H, W)
+    template[...] = averaged[...]
 
 
 def shards(volumes, depth_shift, plane_shift, fraction_steps):
@@ -433,17 +427,15 @@
         pltpu.VMEM((5 * U * NF, W), F32),
         pltpu.VMEM((U * NF, W), F32),
         pltpu.VMEM((3, 2 * B, NF, W), BF16),
-        pltpu.VMEM((3, B, H + 2 * PAD, W), BF16),
         pltpu.VMEM((3, B, H, W), BF16),
         pltpu.VMEM((2 * W, W), BF16),
         pltpu.VMEM((3 * W, W), BF16),
-        pltpu.VMEM((W, W), BF16),
         pltpu.VMEM((W, W), BF16),
         pltpu.SemaphoreType.DMA((C, 11)),
         pltpu.SemaphoreType.DMA((C, 11)),
         pltpu.SemaphoreType.DMA((2 * C + 1,)),
     ]
-    velocity, template = pl.pallas_call(
+    along, averaged = pl.pallas_call(
         kernel,
         out_shape=(jax.ShapeDtypeStruct((3, B, H, W), BF16), jax.ShapeDtypeStruct((B, H, W), BF16)),
         in_specs=[anywhere, smem, smem, smem],
@@ -452,6 +444,17 @@
         compiler_params=pltpu.CompilerParams(
             collective_id=0, has_side_effects=True, vmem_limit_bytes=56 * 1024 * 1024),
     )(volumes[0], depth_shift.reshape(1), plane_shift.reshape(2), fraction_steps.reshape(3))
+    three = pl.BlockSpec((3, Z, H, W), lambda z: (0, z, 0, 0))
+    one = pl.BlockSpec((Z, H, W), lambda z: (z, 0, 0))
+    velocity, template = pl.pallas_call(
+        smooth_in_plane,
+        grid=(B // Z,),
+        out_shape=(jax.ShapeDtypeStruct((3, B, H, W), BF16), jax.ShapeDtypeStruct((B, H, W), BF16)),
+        in_specs=[three, one],
+        out_specs=(three, one),
+        scratch_shapes=[pltpu.VMEM((W, W), BF16)],
+        compiler_params=pltpu.CompilerParams(vmem_limit_bytes=60 * 1024 * 1024),
+    )(along, averaged)
     return velocity[None], template
 
 

time: 101 us -> 95.6 us (0.947)
  local copies, waits for them, and re-layouts: 4.92 us -> 0 us
    pallas_call x1, Pallas kernels: 93.6 us -> 88.3 us  [shards(): pl.pallas_call(kernel, out_shape=(jax.ShapeDtypeStruct((3, B, H, W), BF16...]
    pallas_call x0 -> x1, Pallas kernels: none -> 4.93 us  [shards(): pl.pallas_call(smooth_in_plane, grid=(B // Z,), out_shape=(jax.ShapeDtype...]
    unnamed x4 -> x0, local copies, waits for them, and re-layouts: 4.92 us -> none
where the time goes in v4:
time: 95.6 us; the launch traced here: 94.5 us
  Pallas kernels  93.2 us (97%)
  between operations  1.28 us (1%)
    pallas_call x1, Pallas kernels, shards(): pl.pallas_call(kernel, out_shape=(jax.ShapeDtypeStruct((3, B, H, W), BF16...  88.3 us
    pallas_call x1, Pallas kernels, shards(): pl.pallas_call(smooth_in_plane, grid=(B // Z,), out_shape=(jax.ShapeDtype...  4.93 us

profile of v4, /device:TPU:8, one launch (start us, length us, event | category | flops | bytes accessed | tf_op | source)
XLA Modules:
  0.0 94.5 jit_solution(10413350532891668258)
XLA Ops:
  1.3 88.3 %shard_map.59 = (bf16[3,8,256,256]{3,2,1,0:T(8,128)(2,1)}, bf16[8,256,256]{2,1,0:T(8,128)(2,1)}) custom-call(bf16[8,256,256]{2,1,0:T(8,128)(2,1)} %bitcast.6, s32[1]{0:T(128)} %bitcast.5.dsh, s32[2]{0:T(128)} %bitcast.7, s32[3]{0:T(128)} %bitcast.8), custom_call_target="tpu_custom_call" | custom-call | tf_op jit(solution)/shard_map/pallas_call | solution.py:438
  89.5 4.9 %shard_map.60 = (bf16[3,8,256,256]{3,2,1,0:T(8,128)(2,1)}, bf16[8,256,256]{2,1,0:T(8,128)(2,1)}) custom-call(bf16[3,8,256,256]{3,2,1,0:T(8,128)(2,1)} %get-tuple-element.6.along, bf16[8,256,256]{2,1,0:T(8,128)(2,1)} %get-tuple-element.7.averaged), custom_call_target="tpu_custom_call" | custom-call | tf_op jit(solution)/shard_map/pallas_call | solution.py:449

commit v5 on v4

--- a/solution.py
+++ b/solution.py
@@ -15,7 +15,7 @@
 NE = B + 2 * HALO
 PAD = 16
 EPS = 1e-5
-SRC = (0, 48, 96, 144, 192, 240, 256)
+SRC = (0, 48, 96, 144, 176, 208, 240, 256)
 C = len(SRC) - 1
 
 
@@ -359,11 +359,17 @@
             ('r', 3),
             ('t', 4),
             ('f', 3),
+            ('s', 6),
+            ('c', 6),
+            ('w', 6),
             ('r', 4),
             ('t', 5),
             ('f', 4),
             ('r', 5),
-            ('f', 5)):
+            ('t', 6),
+            ('f', 5),
+            ('r', 6),
+            ('f', 6)):
         if step == "s":
             own_copy(p).wait()
             landed(p, SRC_R, SRC_L)

time: 95.6 us -> 100 us (1.046)
  Pallas kernels: 93.2 us -> 97.3 us
    pallas_call x1, Pallas kernels: 88.3 us -> 92.4 us  [shards(): pl.pallas_call(kernel, out_shape=(jax.ShapeDtypeStruct((3, B, H, W), BF16...]
where the time goes in v5:
time: 100 us; the launch traced here: 98.6 us
  Pallas kernels  97.3 us (97%)
  between operations  1.28 us (1%)
    pallas_call x1, Pallas kernels, shards(): pl.pallas_call(kernel, out_shape=(jax.ShapeDtypeStruct((3, B, H, W), BF16...  92.4 us
    pallas_call x1, Pallas kernels, shards(): pl.pallas_call(smooth_in_plane, grid=(B // Z,), out_shape=(jax.ShapeDtype...  4.93 us

profile of v5, /device:TPU:8, one launch (start us, length us, event | category | flops | bytes accessed | tf_op | source)
XLA Modules:
  0.0 98.6 jit_solution(9586847161563285761)
XLA Ops:
  1.3 92.4 %shard_map.59 = (bf16[3,8,256,256]{3,2,1,0:T(8,128)(2,1)}, bf16[8,256,256]{2,1,0:T(8,128)(2,1)}) custom-call(bf16[8,256,256]{2,1,0:T(8,128)(2,1)} %bitcast.6, s32[1]{0:T(128)} %bitcast.5.dsh, s32[2]{0:T(128)} %bitcast.7, s32[3]{0:T(128)} %bitcast.8), custom_call_target="tpu_custom_call" | custom-call | tf_op jit(solution)/shard_map/pallas_call | solution.py:444
  93.7 4.9 %shard_map.60 = (bf16[3,8,256,256]{3,2,1,0:T(8,128)(2,1)}, bf16[8,256,256]{2,1,0:T(8,128)(2,1)}) custom-call(bf16[3,8,256,256]{3,2,1,0:T(8,128)(2,1)} %get-tuple-element.6.along, bf16[8,256,256]{2,1,0:T(8,128)(2,1)} %get-tuple-element.7.averaged), custom_call_target="tpu_custom_call" | custom-call | tf_op jit(solution)/shard_map/pallas_call | solution.py:455
